TPU v7x, 32 devices: a whole 2x2x4 slice. The times are simulated.
32 devices in a mesh: bx: 8 (over y, x, core), cy: 4 (over z).
Axes of the slice: x: 2, y: 2, z: 4, core: 2. Of those that a mesh axis runs over, the one named last changes fastest.
Arguments:
- fractions: bfloat16 [8, 256, 16, 512], P(None, 'bx', None, 'cy'), may hold values from 0.05 to 1134.4, as said below
- ext_table: bfloat16 [32, 8], replicated, may hold values from 0.5 to 3.5
- side_table: bfloat16 [32, 8], replicated, may hold values from 0.049804688 to 0.59765625
- depth_scale: float32 [32], replicated, may hold values from 3.125e-05 to 0.0026666667, as said below
Outputs:
- image_out: float32 [32, 256, 16], P('cy', 'bx')
Inputs may be any that keep to these rules, and one draw needn't show every extreme that they name: Positive volume fractions. `depth_scale`: positive scales.
All inputs are finite; a program needn't handle non-finite values.
Results may differ from a plain program's by a relative error of at most 0.0003.
Values sent between devices are 32-bit elements; how exact they have to be, the bound alone decides.
A program may use at most 128 MiB of HBM per device.

v0:
```python
import jax
import jax.numpy as jnp
from jax import lax
from jax.sharding import PartitionSpec as P

W = 32
NB = 8


def prefix(part, axis, combine, identity, reverse):
    count = lax.axis_size(axis)
    place = lax.axis_index(axis)
    ahead = count - 1 - place if reverse else place
    gathered = lax.all_gather(part, axis)
    state = jnp.zeros_like(part) + jnp.asarray(identity, part.dtype)

    def one(step, state):
        source = count - 1 - step if reverse else step
        return combine(state, lax.dynamic_index_in_dim(gathered, source, 0, False))

    return lax.fori_loop(0, ahead, one, state)


def add_planes(earlier, later):
    return earlier + later


def on_device(fractions, ext_table, side_table, depth_scale):
    tables = jnp.concatenate([ext_table, side_table], axis=0)
    cells_x = fractions.shape[1]
    cells_z = fractions.shape[2]
    cells_y = fractions.shape[3]
    total_y = cells_y * lax.axis_size("cy")
    stacked = jnp.dot(tables, fractions.reshape(NB, -1), preferred_element_type=jnp.float32)
    stacked = stacked.reshape(2 * W, cells_x, cells_z, cells_y)
    extinction = stacked[:W] * depth_scale[:, None, None, None]
    side_light = stacked[W:]
    x_index = jnp.arange(cells_x, dtype=jnp.int32)
    y_index = jnp.arange(cells_y, dtype=jnp.int32)
    lower_ones = (x_index[:, None] <= x_index[None, :]).astype(jnp.float32)
    upper_ones = (y_index[:, None] >= y_index[None, :]).astype(jnp.float32)
    along_x = jnp.einsum("wxzy,xk->wkzy", extinction, lower_ones, precision=lax.Precision.HIGHEST)
    along_y = jnp.einsum("wxzy,yk->wxzk", extinction, upper_ones, precision=lax.Precision.HIGHEST)
    beam_totals = along_x[:, -1]
    zero_plane = jnp.zeros(beam_totals.shape, jnp.float32)
    carried = prefix(beam_totals, "bx", add_planes, zero_plane, False)
    beam_depth = carried[:, None] + along_x - 0.5 * extinction
    local_camera = along_y - 0.5 * extinction
    camera_totals = along_y[:, :, :, 0]
    partial_image = jnp.sum(side_light * jnp.exp(-(beam_depth + local_camera)), axis=3) / total_y
    zero_image = jnp.zeros(camera_totals.shape, jnp.float32)
    camera_carried = prefix(camera_totals, "cy", add_planes, zero_image, True)
    image_out = lax.psum_scatter(
        partial_image * jnp.exp(-camera_carried), "cy", scatter_dimension=0, tiled=True
    )
    return image_out


def solution(mesh):
    return jax.shard_map(
        on_device,
        mesh=mesh,
        in_specs=(P(None, "bx", None, "cy"), P(), P(), P()),
        out_specs=P("cy", "bx", None),
        check_vma=False,
    )
```

profile of v0, /device:TPU:0, one launch (start us, length us, event | category | flops | bytes accessed | tf_op | source)
XLA Modules:
  0.0 140.0 jit_solution(9608977540597793436)
XLA Ops:
  6.5 0.0 all-gather.4.cloned.1.call-start
  6.5 3.7 %fusion.6 = f32[64,65536]{1,0:T(8,128)S(1)} fusion(bf16[1,8,512,128]{3,2,1,0:T(8,128)(2,1)} %bitcast.43, bf16[32,8]{0,1:T(8,128)(2,1)} %param.10, bf16[32,8]{0,1:T(8,128)(2,1)} %param.9), kind=kOutput, calls=%fused_computation.14 | convolution fusion | flops 67110912 | bytes 17826816 | tf_op jit(solution)/shard_map/dot_general | solution.py:34
  10.2 6.5 %slice_bitcast_fusion.1 = (f32[4,8,512,128]{3,1,2,0:T(8,128)}, f32[4,8,512,128]{3,1,2,0:T(8,128)}) fusion(f32[64,65536]{1,0:T(8,128)S(1)} %fusion.6), kind=kLoop, calls=%fused_computation.3 | loop fusion | bytes 33554432
  16.7 4.9 %copy.29 = f32[4,8,512,128]{3,2,1,0:T(8,128)S(1)} copy(f32[4,8,512,128]{3,1,2,0:T(8,128)} %get-tuple-element.115) | data formatting | bytes 16777216
  21.6 4.1 %copy_multiply_fusion.1 = f32[32,32,16,128]{3,1,2,0:T(8,128)S(1)} fusion(f32[32,32,16,128]{3,2,1,0:T(8,128)S(1)} %bitcast.38, f32[32]{0:T(128)S(1)} %copy-done.3), kind=kLoop, calls=%fused_computation.12 | loop fusion | flops 2097152 | bytes 16777344 | tf_op jit(solution)/shard_map/mul | solution.py:36
  25.7 4.6 %convolution_bitcast_fusion = f32[32,32,16,128]{3,1,2,0:T(8,128)S(1)} fusion(f32[32,32,16,128]{3,1,2,0:T(8,128)S(1)} %copy_multiply_fusion.1), kind=kOutput, calls=%fused_computation.13 | convolution fusion | flops 805307392 | bytes 16777216 | tf_op jit(solution)/shard_map/wxzy,xk->wkzy/dot_general | solution.py:42
  30.3 3.2 %copy-done.2 = f32[32,32,16,128]{3,1,2,0:T(8,128)} copy-done((f32[32,32,16,128]{3,1,2,0:T(8,128)}, f32[32,32,16,128]{3,1,2,0:T(8,128)S(1)}, u32[]{:S(2)}) %copy-start.2) | copy-done | bytes 8388632
  33.5 1.0 slice.26
  34.5 0.0 copy-done.1
  34.5 0.0 all-gather.4.cloned.1.call-update
  34.6 0.0 reduce-scatter.2.cloned.1.call-start
  34.6 13.9 %fusion.4 = f32[32,32,16,128]{3,2,1,0:T(8,128)} fusion(f32[32,32,16,128]{3,1,2,0:T(8,128)} %copy-done.1), kind=kOutput, calls=%fused_computation.10 | convolution fusion | flops 3221241856 | bytes 16777216 | tf_op jit(solution)/shard_map/wxzy,yk->wxzk/dot_general | solution.py:43
  48.5 5.9 %copy.21 = f32[32,32,16,1]{1,2,3,0:T(8,128)S(1)} copy(f32[32,32,16,1]{3,2,1,0:T(8,128)} %bitcast.40) | data formatting | bytes 131072 | tf_op jit(solution)/shard_map/slice | solution.py:49
  54.4 8.4 %copy.28 = f32[4,8,512,128]{3,2,1,0:T(8,128)} copy(f32[4,8,512,128]{3,1,2,0:T(8,128)} %get-tuple-element.114) | data formatting | bytes 16777216
  62.9 23.8 %all-gather.1 = f32[128,32,16,1]{1,2,3,0:T(8,128)S(1)} all-gather(f32[32,32,16,1]{1,2,3,0:T(8,128)S(1)} %copy.21), channel_id=3, replica_groups=mesh['bx'=8,'cy'=4] {'cy'}, dimensions={0}, use_global_device_ids=true | all-gather | bytes 327680 | tf_op jit(solution)/shard_map/all_gather | solution.py:14
  86.7 0.2 while.23
  86.7 0.1 bitcast_add_fusion.5
  86.8 0.1 bitcast_add_fusion.5
  86.9 0.1 bitcast_add_fusion.5
  87.0 0.0 all-gather.4.cloned.1.call-done
  87.0 19.3 %fusion = f32[32,32,16]{1,2,0:T(8,128)S(1)} fusion(f32[32,32,16,128]{3,2,1,0:T(8,128)} %bitcast.41, f32[32,32,16,128]{3,2,1,0:T(8,128)} %fusion.4, f32[32,32,16,128]{3,1,2,0:T(8,128)} %copy-done.2, f32[32,16,128]{2,1,0:T(8,128)S(1)} %get-tuple-element.84, f32[32]{0:T(128)S(1)} %copy-done.3, f32[32,32,16,128]{3,2,1,0:T(8,128)} %bitcast.39), kind=kLoop, calls=%fused_computation.5 | loop fusion | flops 18857984 | bytes 33882240 | tf_op jit(solution)/shard_map/reduce_sum | solution.py:50
  106.4 0.7 exponential_multiply_fusion
  107.1 0.0 reduce-scatter.2.cloned.1.call-update
  107.1 26.0 %reduce-scatter.2.cloned.1.call-done = f32[8,32,16]{1,2,0:T(8,128)} async-done(((f32[32,32,16]{1,2,0:T(8,128)}), f32[8,32,16]{1,2,0:T(8,128)}) %reduce-scatter.2.cloned.1.call-update) | async-done | bytes 16400 | tf_op jit(solution)/shard_map/reduce_scatter | solution.py:53
  (9 shorter events, 0.1 us)
Async XLA Ops:
  6.5 80.4 %all-gather.4.cloned.1.call-start = ((), (), s32[]{:S(2)}) async-start(), calls=%async_computation.2 | async-start | bytes 2359296 | tf_op jit(solution)/shard_map/all_gather | solution.py:14
  16.7 4.9 %copy-start.3 = (f32[32]{0:T(128)S(1)}, f32[32]{0:T(128)}, u32[]{:S(2)}) copy-start(f32[32]{0:T(128)} %param.11) | copy-start | bytes 388
  21.6 4.1 %copy-start = (f32[4,8,512,128]{3,2,1,0:T(8,128)}, f32[4,8,512,128]{3,2,1,0:T(8,128)S(1)}, u32[]{:S(2)}) copy-start(f32[4,8,512,128]{3,2,1,0:T(8,128)S(1)} %copy.29) | copy-start | bytes 25165828
  25.7 8.8 %copy-start.1 = (f32[32,32,16,128]{3,1,2,0:T(8,128)}, f32[32,32,16,128]{3,1,2,0:T(8,128)S(1)}, u32[]{:S(2)}) copy-start(f32[32,32,16,128]{3,1,2,0:T(8,128)S(1)} %copy_multiply_fusion.1) | copy-start | bytes 25165828
  30.3 3.2 %copy-start.2 = (f32[32,32,16,128]{3,1,2,0:T(8,128)}, f32[32,32,16,128]{3,1,2,0:T(8,128)S(1)}, u32[]{:S(2)}) copy-start(f32[32,32,16,128]{3,1,2,0:T(8,128)S(1)} %convolution_bitcast_fusion) | copy-start | bytes 25165828
  34.6 98.6 %reduce-scatter.2.cloned.1.call-start = ((), (), s32[]{:S(2)}) async-start(), calls=%async_computation.1 | async-start | bytes 327680 | tf_op jit(solution)/shard_map/reduce_scatter | solution.py:53
Sparse Core Ops, SparseCore 0:
  34.7 30.5 all-gather.3
  107.2 25.8 reduce-scatter.1
where the time goes:
time: 140 us
  local copies, waits for them, and re-layouts  29.9 us (21%)
  waiting for transfers between devices  26 us (19%)
  other arithmetic  24.3 us (17%)
  blocking collectives  23.8 us (17%)
  matrix products  22.2 us (16%)
  between operations  13.5 us (10%)
    reduce_scatter x1, waiting for transfers between devices, on_device(): lax.psum_scatter(partial_image * jnp.exp(-camera_carried), 'cy', scatter_...  26 us
    all_gather x1, blocking collectives, prefix(): gathered = lax.all_gather(part, axis)  23.8 us
    unnamed x11, local copies, waits for them, and re-layouts  23 us
    reduce_sum x1, other arithmetic, on_device(): jnp.sum(side_light * jnp.exp(-(beam_depth + local_camera)), axis=3)  19.3 us
    dot_general x1, matrix products, on_device(): jnp.einsum('wxzy,yk->wxzk', extinction, upper_ones, precision=lax.Precisi...  13.9 us
    slice x1, local copies, waits for them, and re-layouts, on_device(): camera_totals = along_y[:, :, :, 0]  5.88 us
    dot_general x1, matrix products, on_device(): jnp.einsum('wxzy,xk->wkzy', extinction, lower_ones, precision=lax.Precisi...  4.59 us
    mul x1, other arithmetic, on_device(): extinction = stacked[:W] * depth_scale[:, None, None, None]  4.05 us
  transfers between devices with their start and end apart: 2, of which 1 were waited for; matrix products, arithmetic and copies ran while one was open for 20% of the time, Pallas kernels for 0%

commit v1 on v0

v1 whole, which is shorter than its diff:
```python
import functools

import jax
import jax.numpy as jnp
from jax import lax
from jax.experimental import pallas as pl
from jax.experimental.pallas import tpu as pltpu
from jax.sharding import PartitionSpec as P

LOG2E = 1.4426950408889634
MESH = pl.DeviceIdType.MESH


def split_halves(value):
    high = value.astype(jnp.bfloat16)
    low = (value - high.astype(jnp.float32)).astype(jnp.bfloat16)
    return jnp.concatenate([high, low], axis=1)


def matmul(a, b, dims=((1,), (0,))):
    return lax.dot_general(a, b, (dims, ((), ())), preferred_element_type=jnp.float32)


def kernel(
    n, m, f_hbm, ext_ref, side_ref, scale_ref, out_ref,
    f_ref, prod_ref, beam_ref, beam_in, cam_ref, cam_in, img_ref, img_out, img_in,
    ext_w, side_w, factor_ref,
    f_sem, beam_send, beam_recv, cam_send, cam_recv, img_send, img_recv,
):
    nb, cx, nz, cy = f_ref.shape
    w = ext_ref.shape[1]
    bz, wz = nb * nz, w * nz
    bx_me, cy_me = lax.axis_index("bx"), lax.axis_index("cy")

    load = pltpu.make_async_copy(f_hbm, f_ref, f_sem)
    load.start()

    barrier = pltpu.get_barrier_semaphore()

    def greet_bx(t, c):
        pl.semaphore_signal(barrier, inc=1, device_id={"bx": t}, device_id_type=MESH)
        return c

    def greet_cy(t, c):
        @pl.when(t != cy_me)
        def _():
            pl.semaphore_signal(barrier, inc=1, device_id={"cy": t}, device_id_type=MESH)
        return c

    lax.fori_loop(0, bx_me, greet_bx, 0)
    lax.fori_loop(0, m, greet_cy, 0)

    i32, bf16, f32 = jnp.int32, jnp.bfloat16, jnp.float32
    lane_w = lax.broadcasted_iota(i32, (w, wz), 1) // nz
    spread = (lane_w == lax.broadcasted_iota(i32, (w, wz), 0)).astype(f32)
    row_b = lax.broadcasted_iota(i32, (bz, nb), 0) // nz
    rows = (row_b == lax.broadcasted_iota(i32, (bz, nb), 1)).astype(f32).astype(bf16)
    same_z = (
        lax.broadcasted_iota(i32, (bz, wz), 0) % nz
        == lax.broadcasted_iota(i32, (bz, wz), 1) % nz
    )
    spread16 = spread.astype(bf16)

    def table(ref):
        wide = matmul(rows, matmul(ref[...], spread16).astype(bf16))
        return jnp.where(same_z, wide, 0.0).astype(bf16)

    ext = table(ext_ref)
    ext_w[:bz] = ext
    ext_w[bz:] = ext
    side_w[...] = table(side_ref)
    scale = lax.dot_general(
        jnp.broadcast_to(scale_ref[...], (8, w)), spread, (((1,), (0,)), ((), ())),
        precision=lax.Precision.HIGHEST, preferred_element_type=f32,
    )
    factor_ref[...] = scale * (-LOG2E)

    load.wait()

    def add_x(x, total):
        return total + f_ref[:, x].astype(f32)

    total = lax.fori_loop(0, cx, add_x, jnp.zeros((nb, nz, cy), f32), unroll=4)
    beam_ref[...] = total.reshape(bz, cy)

    pl.semaphore_wait(barrier, n - 1 - bx_me + m - 1)

    def beam_copy(slot, t):
        return pltpu.make_async_remote_copy(
            src_ref=beam_ref, dst_ref=beam_in.at[slot],
            send_sem=beam_send.at[t], recv_sem=beam_recv.at[slot],
            device_id={"bx": t}, device_id_type=MESH,
        )

    def beam_start(t, c):
        beam_copy(bx_me, t).start()
        return c

    lax.fori_loop(bx_me + 1, n, beam_start, 0)

    r = lax.broadcasted_iota(i32, (2 * cy, cy), 0)
    y = lax.broadcasted_iota(i32, (2 * cy, cy), 1)
    above = jnp.where(y >= r, 1.0, 0.0)
    sums = jnp.where(r < cy, above, jnp.where(y == r - cy, 1.0, 0.0)).astype(bf16)

    def two_x(i, before):
        pair = jnp.concatenate(
            [f_ref[:, 2 * i].reshape(bz, cy), f_ref[:, 2 * i + 1].reshape(bz, cy)], axis=0
        )
        both = matmul(sums, pair, ((1,), (1,)))
        for k in range(2):
            x = 2 * i + k
            camera = both[:cy, k * bz:(k + 1) * bz]
            cells = both[cy:, k * bz:(k + 1) * bz]
            cam_ref[pl.ds(x, 1), :] = camera[:1]
            depth = matmul(split_halves(camera + before), ext_w[...])
            light = matmul(cells.astype(bf16), side_w[...])
            prod_ref[x] = light * jnp.exp2(depth * factor_ref[:1])
            before = before + cells
        return before

    lax.fori_loop(0, cx // 2, two_x, jnp.zeros((cy, bz), f32))

    def cam_copy(slot, t):
        return pltpu.make_async_remote_copy(
            src_ref=cam_ref, dst_ref=cam_in.at[slot],
            send_sem=cam_send.at[t], recv_sem=cam_recv.at[slot],
            device_id={"cy": t}, device_id_type=MESH,
        )

    def cam_start(t, c):
        cam_copy(cy_me, t).start()
        return c

    lax.fori_loop(0, cy_me, cam_start, 0)

    def beam_add(j, total):
        beam_copy(j, j).wait_recv()
        return total + beam_in[j]

    beam = lax.fori_loop(0, bx_me, beam_add, jnp.zeros((bz, cy), f32))
    beam_depth = matmul(split_halves(beam.T), ext_w[...])
    beam_factor = jnp.exp2(beam_depth * factor_ref[:1])
    prod_dim = 128
    for lane in range(0, wz, prod_dim):
        lanes = slice(lane, lane + prod_dim)
        part = beam_factor[:, lanes]

        def eight_x(g, c):
            first = pl.multiple_of(8 * g, 8)
            rows8 = [
                jnp.sum(prod_ref[first + k, :, lanes] * part, axis=0, keepdims=True)
                for k in range(8)
            ]
            img_ref[pl.ds(first, 8), lanes] = jnp.concatenate(rows8, axis=0)
            return c

        lax.fori_loop(0, cx // 8, eight_x, 0)

    def cam_add(j, total):
        cam_copy(j, j).wait_recv()
        return total + cam_in[j]

    cam = lax.fori_loop(cy_me + 1, m, cam_add, jnp.zeros((cx, bz), f32))
    cam_depth = matmul(split_halves(cam), ext_w[...])
    image = img_ref[...] * jnp.exp2(cam_depth * factor_ref[:1]) * (1.0 / (cy * m))
    width = wz // m
    for j in range(m):
        img_out[j] = image[:, j * width:(j + 1) * width]

    def img_copy(block, slot, t):
        return pltpu.make_async_remote_copy(
            src_ref=img_out.at[block], dst_ref=img_in.at[slot],
            send_sem=img_send.at[t], recv_sem=img_recv.at[slot],
            device_id={"cy": t}, device_id_type=MESH,
        )

    def img_start(t, c):
        @pl.when(t != cy_me)
        def _():
            img_copy(t, cy_me, t).start()
        return c

    lax.fori_loop(0, m, img_start, 0)
    out_ref[...] = img_out[cy_me]

    def img_add(j, c):
        @pl.when(j != cy_me)
        def _():
            img_copy(j, j, j).wait_recv()
            out_ref[...] += img_in[j]
        return c

    lax.fori_loop(0, m, img_add, 0)

    def beam_sent(t, c):
        beam_copy(bx_me, t).wait_send()
        return c

    def cam_sent(t, c):
        cam_copy(cy_me, t).wait_send()
        return c

    def img_sent(t, c):
        @pl.when(t != cy_me)
        def _():
            img_copy(t, cy_me, t).wait_send()
        return c

    lax.fori_loop(bx_me + 1, n, beam_sent, 0)
    lax.fori_loop(0, cy_me, cam_sent, 0)
    lax.fori_loop(0, m, img_sent, 0)


def on_device(n, m, fractions, ext_table, side_table, depth_scale):
    nb, cx, nz, cy = fractions.shape
    w = ext_table.shape[0]
    bz, wz = nb * nz, w * nz
    width = wz // m
    f32, bf16 = jnp.float32, jnp.bfloat16
    dma = pltpu.SemaphoreType.DMA
    vmem = pl.BlockSpec(memory_space=pltpu.VMEM)
    image = pl.pallas_call(
        functools.partial(kernel, n, m),
        out_shape=jax.ShapeDtypeStruct((cx, width), f32),
        in_specs=[pl.BlockSpec(memory_space=pl.ANY), vmem, vmem, vmem],
        out_specs=vmem,
        scratch_shapes=[
            pltpu.VMEM((nb, cx, nz, cy), bf16),
            pltpu.VMEM((cx, cy, wz), f32),
            pltpu.VMEM((bz, cy), f32),
            pltpu.VMEM((n, bz, cy), f32),
            pltpu.VMEM((cx, bz), f32),
            pltpu.VMEM((m, cx, bz), f32),
            pltpu.VMEM((cx, wz), f32),
            pltpu.VMEM((m, cx, width), f32),
            pltpu.VMEM((m, cx, width), f32),
            pltpu.VMEM((2 * bz, wz), bf16),
            pltpu.VMEM((bz, wz), bf16),
            pltpu.VMEM((8, wz), f32),
            dma, dma((n,)), dma((n,)), dma((m,)), dma((m,)), dma((m,)), dma((m,)),
        ],
        compiler_params=pltpu.CompilerParams(
            collective_id=0, has_side_effects=True, vmem_limit_bytes=40 * 1024 * 1024
        ),
    )(fractions, ext_table.T, side_table.T, depth_scale.reshape(1, w))
    return jnp.transpose(image.reshape(cx, w // m, nz), (1, 0, 2))


def solution(mesh):
    return jax.shard_map(
        functools.partial(on_device, mesh.shape["bx"], mesh.shape["cy"]),
        mesh=mesh,
        in_specs=(P(None, "bx", None, "cy"), P(), P(), P()),
        out_specs=P("cy", "bx", None),
        check_vma=False,
    )
```

time: 140 us -> 22.7 us (0.16)
  local copies, waits for them, and re-layouts: 29.9 us -> 2.65 us
  waiting for transfers between devices: 26 us -> 0 us
  other arithmetic: 24.3 us -> 0 us
  blocking collectives: 23.8 us -> 0 us
  matrix products: 22.2 us -> 0 us
  Pallas kernels: 0 us -> 19.8 us
  between operations: 13.5 us -> 0.01 us
    reduce_scatter x1 -> x0, waiting for transfers between devices: 26 us -> none  [on_device(): lax.psum_scatter(partial_image * jnp.exp(-camera_carried), 'cy', scatter_...]
    all_gather x1 -> x0, blocking collectives: 23.8 us -> none  [prefix(): gathered = lax.all_gather(part, axis)]
    dot_general x3 -> x0, matrix products: 22.2 us -> none  [the longest x1 13.9 us: on_device(): jnp.einsum('wxzy,yk->wxzk', extinction, upper_ones, precision=lax.Precisi...]
    unnamed x11 -> x8, local copies, waits for them, and re-layouts: 23 us -> 1.92 us
    pallas_call x0 -> x1, Pallas kernels: none -> 19.8 us  [on_device(): pl.pallas_call(functools.partial(kernel, n, m), out_shape=jax.ShapeDtypeS...]
    reduce_sum x1 -> x0, other arithmetic: 19.3 us -> none  [on_device(): jnp.sum(side_light * jnp.exp(-(beam_depth + local_camera)), axis=3)]
    slice x2 -> x0, local copies, waits for them, and re-layouts: 6.87 us -> none  [the longest x1 5.88 us: on_device(): camera_totals = along_y[:, :, :, 0]]
    mul x2 -> x0, other arithmetic: 4.8 us -> none  [the longest x1 4.05 us: on_device(): extinction = stacked[:W] * depth_scale[:, None, None, None]]
  transfers between devices with their start and end apart: 2 -> 0, of which waited for: 1 -> 0; matrix products, arithmetic and copies ran while one was open for 20% -> 0% of each run, Pallas kernels for 0% -> 0%
where the time goes in v1:
time: 22.7 us; the launch traced here: 22.5 us
  Pallas kernels  19.8 us (87%)
  local copies, waits for them, and re-layouts  2.65 us (12%)
    pallas_call x1, Pallas kernels, on_device(): pl.pallas_call(functools.partial(kernel, n, m), out_shape=jax.ShapeDtypeS...  19.8 us
    unnamed x8, local copies, waits for them, and re-layouts  1.92 us
    pallas_call x1, local copies, waits for them, and re-layouts, on_device(): pl.pallas_call(functools.partial(kernel, n, m), out_shape=jax.ShapeDtypeS...  0.73 us

profile of v1, /device:TPU:0, one launch (start us, length us, event | category | flops | bytes accessed | tf_op | source)
XLA Modules:
  0.0 22.5 jit_solution(13382435478498552688)
XLA Ops:
  0.0 0.0 copy-start.2
  0.0 0.0 copy-start.1
  0.0 0.0 copy-start.3
  0.0 0.7 %copy-done.2 = bf16[32,8]{0,1:T(8,128)(2,1)S(1)} copy-done((bf16[32,8]{0,1:T(8,128)(2,1)S(1)}, bf16[32,8]{0,1:T(8,128)(2,1)}, u32[]{:S(2)}) %copy-start.2) | copy-done | bytes 536
  0.7 0.0 copy-done.1
  0.7 0.0 copy-done.3
  0.7 0.0 copy-start
  0.7 1.2 %copy-done = bf16[8,32,16,128]{3,2,1,0:T(8,128)(2,1)S(1)} copy-done((bf16[8,32,16,128]{3,2,1,0:T(8,128)(2,1)S(1)}, bf16[8,32,16,128]{3,2,1,0:T(8,128)(2,1)}, u32[]{:S(2)}) %copy-start) | copy-done | bytes 1048600
  1.9 19.8 %shard_map.46 = f32[32,128]{1,0:T(8,128)S(1)} custom-call(bf16[8,32,16,128]{3,2,1,0:T(8,128)(2,1)S(1)} %copy-done, bf16[8,32]{1,0:T(8,128)(2,1)S(1)} %bitcast.6, bf16[8,32]{1,0:T(8,128)(2,1)S(1)} %bitcast.7, f32[1,32]{1,0:T(1,128)S(1)} %bitcast.8), custom_call_target="tpu_custom_call" | custom-call | tf_op jit(solution)/shard_map/pallas_call | solution.py:223
  21.8 0.7 %copy.6 = f32[32,128]{0,1:T(8,128)} copy(f32[32,128]{1,0:T(8,128)S(1)} %shard_map.46) | data formatting | bytes 32768 | tf_op jit(solution)/shard_map/pallas_call | solution.py:223
Async XLA Ops:
  0.0 0.7 %copy-start.2 = (bf16[32,8]{0,1:T(8,128)(2,1)S(1)}, bf16[32,8]{0,1:T(8,128)(2,1)}, u32[]{:S(2)}) copy-start(bf16[32,8]{0,1:T(8,128)(2,1)} %param.6) | copy-start | bytes 1540
  0.0 0.7 %copy-start.1 = (bf16[32,8]{0,1:T(8,128)(2,1)S(1)}, bf16[32,8]{0,1:T(8,128)(2,1)}, u32[]{:S(2)}) copy-start(bf16[32,8]{0,1:T(8,128)(2,1)} %param.5) | copy-start | bytes 1540
  0.0 0.7 %copy-start.3 = (f32[32]{0:T(128)S(1)}, f32[32]{0:T(128)}, u32[]{:S(2)}) copy-start(f32[32]{0:T(128)} %param.7) | copy-start | bytes 388
  0.7 1.2 %copy-start = (bf16[8,32,16,128]{3,2,1,0:T(8,128)(2,1)S(1)}, bf16[8,32,16,128]{3,2,1,0:T(8,128)(2,1)}, u32[]{:S(2)}) copy-start(bf16[8,32,16,128]{3,2,1,0:T(8,128)(2,1)} %f_hbm.1) | copy-start | bytes 3145732

commit v2 on v1

v2 whole, which is shorter than its diff:
```python
import functools

import jax
import jax.numpy as jnp
from jax import lax
from jax.experimental import pallas as pl
from jax.experimental.pallas import tpu as pltpu
from jax.sharding import PartitionSpec as P

LOG2E = 1.4426950408889634
MESH = pl.DeviceIdType.MESH
GROUP = 8
EARLY = 0
FIRST = 1
SECOND = 2
THIRD = 3


def split_halves(value):
    high = value.astype(jnp.bfloat16)
    low = (value - high.astype(jnp.float32)).astype(jnp.bfloat16)
    return jnp.concatenate([high, low], axis=1)


def matmul(a, b, dims=((1,), (0,))):
    return lax.dot_general(a, b, (dims, ((), ())), preferred_element_type=jnp.float32)


def kernel(
    n, m, f_hbm, ext_hbm, side_hbm, scale_hbm, out_ref,
    f_ref, ext_ref, side_ref, scale_ref, prod_ref, beam_ref, mate_in, pair_ref, pair_in, ahead_ref, ahead_in, cam_ref, cam_in, img_ref, img_out, img_in,
    ext_w, side_w, factor_ref,
    f_sem, table_sem, mate_sem, ahead_sem, pair_send, pair_recv, cam_send, cam_recv, img_send, img_recv,
):
    nb, cx, nz, cy = f_ref.shape
    w = ext_ref.shape[1]
    bz, wz = nb * nz, w * nz
    bx_me, cy_me = lax.axis_index("bx"), lax.axis_index("cy")


    barrier = pltpu.get_barrier_semaphore()

    half, pair, pairs = bx_me % 2, bx_me // 2, n // 2
    mate = 2 * pair + 1 - half

    def greet_bx(t, c):
        pl.semaphore_signal(
            barrier, inc=1, device_id={"bx": 2 * t + half}, device_id_type=MESH
        )
        return c

    pl.semaphore_signal(barrier, inc=1, device_id={"bx": mate}, device_id_type=MESH)

    def greet_cy(t, c):
        @pl.when(t != cy_me)
        def _():
            pl.semaphore_signal(barrier, inc=1, device_id={"cy": t}, device_id_type=MESH)
        return c

    lax.fori_loop(0, pair, greet_bx, 0)
    lax.fori_loop(0, m, greet_cy, 0)

    loads = [
        pltpu.make_async_copy(src, dst, table_sem.at[k])
        for k, (src, dst) in enumerate(
            ((ext_hbm, ext_ref), (side_hbm, side_ref), (scale_hbm, scale_ref))
        )
    ]
    load = pltpu.make_async_copy(f_hbm, f_ref, f_sem)
    for copy in (*loads, load):
        copy.start()

    i32, bf16, f32 = jnp.int32, jnp.bfloat16, jnp.float32
    lane_w = lax.broadcasted_iota(i32, (w, wz), 1) // nz
    spread = (lane_w == lax.broadcasted_iota(i32, (w, wz), 0)).astype(f32)
    row_b = lax.broadcasted_iota(i32, (bz, nb), 0) // nz
    rows = (row_b == lax.broadcasted_iota(i32, (bz, nb), 1)).astype(f32).astype(bf16)
    same_z = (
        lax.broadcasted_iota(i32, (bz, wz), 0) % nz
        == lax.broadcasted_iota(i32, (bz, wz), 1) % nz
    )
    spread16 = spread.astype(bf16)

    for copy in loads:
        copy.wait()

    def table(ref):
        wide = matmul(rows, matmul(ref[...], spread16).astype(bf16))
        return jnp.where(same_z, wide, 0.0).astype(bf16)

    ext = table(ext_ref)
    ext_w[:bz] = ext
    ext_w[bz:] = ext
    side_w[...] = table(side_ref)
    scale = lax.dot_general(
        jnp.broadcast_to(scale_ref[...], (8, w)), spread, (((1,), (0,)), ((), ())),
        precision=lax.Precision.HIGHEST, preferred_element_type=f32,
    )
    factor_ref[...] = scale * (-LOG2E)

    load.wait()

    def add_x(x, total):
        return total + f_ref[:, x].astype(f32)

    total = lax.fori_loop(0, cx, add_x, jnp.zeros((nb, nz, cy), f32), unroll=4)
    beam_ref[...] = total.reshape(2, bz // 2, cy)

    r = lax.broadcasted_iota(i32, (2 * cy, cy), 0)
    y = lax.broadcasted_iota(i32, (2 * cy, cy), 1)
    above = jnp.where(y >= r, 1.0, 0.0)
    sums = jnp.where(r < cy, above, jnp.where(y == r - cy, 1.0, 0.0)).astype(bf16)

    ones = jnp.ones((8, cy), bf16)
    for x in range(cx):
        to_camera = matmul(ones, f_ref[:, x].reshape(bz, cy), ((1,), (1,)))
        cam_ref[x:x + 1, :] = to_camera[:1]

    def group(i, before, fused=False):
        first = i * GROUP
        depths, lights = [], []
        for k in range(0, GROUP, 2):
            pair = jnp.concatenate(
                [f_ref[:, first + k].reshape(bz, cy), f_ref[:, first + k + 1].reshape(bz, cy)],
                axis=0,
            )
            both = matmul(sums, pair, ((1,), (1,)))
            for lanes in (slice(0, bz), slice(bz, 2 * bz)):
                cells = both[cy:, lanes]
                depths.append(split_halves(both[:cy, lanes] + before))
                lights.append(cells.astype(bf16))
                before = before + cells
        depth = matmul(jnp.concatenate(depths, axis=0), ext_w[...])
        light = matmul(jnp.concatenate(lights, axis=0), side_w[...])
        product = (light * jnp.exp2(depth * factor_ref[:1])).reshape(GROUP, cy, wz)
        if fused:
            image = jnp.sum(product, axis=1)
            img_ref[pl.ds(pl.multiple_of(first, GROUP), GROUP)] = image
        else:
            prod_ref[pl.ds(first, GROUP)] = product
        return before

    steps = cx // GROUP
    early = EARLY
    before = lax.fori_loop(0, early, group, jnp.zeros((cy, bz), f32))

    pl.semaphore_wait(barrier, pairs - 1 - pair + m)

    def to_mate(src, dst, sem):
        return pltpu.make_async_remote_copy(
            src_ref=src, dst_ref=dst, send_sem=sem.at[0], recv_sem=sem.at[1],
            device_id={"bx": mate}, device_id_type=MESH,
        )

    def pair_copy(slot, t):
        return pltpu.make_async_remote_copy(
            src_ref=pair_ref, dst_ref=pair_in.at[slot],
            send_sem=pair_send.at[t], recv_sem=pair_recv.at[slot],
            device_id={"bx": 2 * t + half}, device_id_type=MESH,
        )

    mate_copy = to_mate(beam_ref.at[1 - half], mate_in, mate_sem)
    mate_copy.start()

    def cam_copy(slot, t):
        return pltpu.make_async_remote_copy(
            src_ref=cam_ref, dst_ref=cam_in.at[slot],
            send_sem=cam_send.at[t], recv_sem=cam_recv.at[slot],
            device_id={"cy": t}, device_id_type=MESH,
        )

    def cam_start(t, c):
        cam_copy(cy_me, t).start()
        return c

    lax.fori_loop(0, cy_me, cam_start, 0)

    before = lax.fori_loop(early, FIRST, group, before)

    mate_copy.wait_recv()
    pair_ref[...] = beam_ref[half] + mate_in[...]

    def pair_start(t, c):
        pair_copy(pair, t).start()
        return c

    lax.fori_loop(pair + 1, pairs, pair_start, 0)
    before = lax.fori_loop(FIRST, SECOND, group, before)

    def pair_add(j, total):
        pair_copy(j, j).wait_recv()
        return total + pair_in[j]

    mine = lax.fori_loop(0, pair, pair_add, jnp.zeros((bz // 2, cy), f32))
    second = jnp.where(half == 1, 1.0, 0.0)
    ahead_ref[...] = mine + (1.0 - second) * beam_ref[half]
    ahead_copy = to_mate(ahead_ref, ahead_in, ahead_sem)
    ahead_copy.start()
    before = lax.fori_loop(SECOND, THIRD, group, before)
    mine = mine + second * mate_in[...]
    ahead_copy.wait_recv()
    other = ahead_in[...]
    beam = jnp.concatenate(
        [jnp.where(half == 0, mine, other), jnp.where(half == 0, other, mine)], axis=0
    )
    def cam_add(j, total):
        cam_copy(j, j).wait_recv()
        return total + cam_in[j]

    cam = lax.fori_loop(cy_me + 1, m, cam_add, jnp.zeros((cx, bz), f32))
    cam_depth = matmul(split_halves(cam), ext_w[...])
    cam_factor = jnp.exp2(cam_depth * factor_ref[:1]) * (1.0 / (cy * m))
    width = wz // m
    edge = cx // 2

    def img_copy(part, block, slot, t):
        return pltpu.make_async_remote_copy(
            src_ref=img_out.at[part, block], dst_ref=img_in.at[part, slot],
            send_sem=img_send.at[part, t], recv_sem=img_recv.at[part, slot],
            device_id={"cy": t}, device_id_type=MESH,
        )

    def img_start(part):
        rows_x = slice(part * edge, (part + 1) * edge)
        image = img_ref[rows_x] * cam_factor[rows_x]
        for j in range(m):
            img_out[part, j] = image[:, j * width:(j + 1) * width]

        def one(t, c):
            @pl.when(t != cy_me)
            def _():
                img_copy(part, t, cy_me, t).start()
            return c

        lax.fori_loop(0, m, one, 0)

    beam_t = beam.T
    lax.fori_loop(
        THIRD, steps, functools.partial(group, fused=True), before + beam_t
    )
    beam_depth = matmul(split_halves(beam_t), ext_w[...])
    beam_factor = jnp.exp2(beam_depth * factor_ref[:1])

    def finish(start, stop):
        for lane in range(0, wz, 128):
            lanes = slice(lane, lane + 128)
            part = beam_factor[:, lanes]

            def eight_x(g, c):
                first = pl.multiple_of(8 * g, 8)
                rows8 = [
                    jnp.sum(prod_ref[first + k, :, lanes] * part, axis=0, keepdims=True)
                    for k in range(8)
                ]
                img_ref[pl.ds(first, 8), lanes] = jnp.concatenate(rows8, axis=0)
                return c

            lax.fori_loop(start // 8, stop // 8, eight_x, 0)

    if THIRD * GROUP > edge:
        finish(edge, THIRD * GROUP)
    img_start(1)
    finish(0, min(edge, THIRD * GROUP))
    img_start(0)
    total_ref = img_out.at[:, cy_me]

    def img_add(j, c):
        @pl.when(j != cy_me)
        def _():
            for part in (1, 0):
                img_copy(part, j, j, j).wait_recv()
            total_ref[...] += img_in[:, j]
        return c

    lax.fori_loop(0, m, img_add, 0)
    image = total_ref[...].reshape(cx, width)
    out_ref[...] = image.T.reshape(out_ref.shape)

    def pair_sent(t, c):
        pair_copy(pair, t).wait_send()
        return c

    mate_copy.wait_send()
    ahead_copy.wait_send()
    def cam_sent(t, c):
        cam_copy(cy_me, t).wait_send()
        return c

    def img_sent(t, c):
        @pl.when(t != cy_me)
        def _():
            for part in range(2):
                img_copy(part, t, cy_me, t).wait_send()
        return c

    lax.fori_loop(pair + 1, pairs, pair_sent, 0)
    lax.fori_loop(0, cy_me, cam_sent, 0)
    lax.fori_loop(0, m, img_sent, 0)


def on_device(n, m, fractions, ext_table, side_table, depth_scale):
    nb, cx, nz, cy = fractions.shape
    w = ext_table.shape[0]
    bz, wz = nb * nz, w * nz
    width = wz // m
    f32, bf16 = jnp.float32, jnp.bfloat16
    dma = pltpu.SemaphoreType.DMA
    vmem = pl.BlockSpec(memory_space=pltpu.VMEM)
    image = pl.pallas_call(
        functools.partial(kernel, n, m),
        out_shape=jax.ShapeDtypeStruct((w // m, nz, cx), f32),
        in_specs=[pl.BlockSpec(memory_space=pltpu.HBM)] * 4,
        out_specs=vmem,
        scratch_shapes=[
            pltpu.VMEM((nb, cx, nz, cy), bf16),
            pltpu.VMEM((nb, w), bf16),
            pltpu.VMEM((nb, w), bf16),
            pltpu.VMEM((1, w), f32),
            pltpu.VMEM((cx, cy, wz), f32),
            pltpu.VMEM((2, bz // 2, cy), f32),
            pltpu.VMEM((bz // 2, cy), f32),
            pltpu.VMEM((bz // 2, cy), f32),
            pltpu.VMEM((n // 2, bz // 2, cy), f32),
            pltpu.VMEM((bz // 2, cy), f32),
            pltpu.VMEM((bz // 2, cy), f32),
            pltpu.VMEM((cx, bz), f32),
            pltpu.VMEM((m, cx, bz), f32),
            pltpu.VMEM((cx, wz), f32),
            pltpu.VMEM((2, m, cx // 2, width), f32),
            pltpu.VMEM((2, m, cx // 2, width), f32),
            pltpu.VMEM((2 * bz, wz), bf16),
            pltpu.VMEM((bz, wz), bf16),
            pltpu.VMEM((8, wz), f32),
            dma, dma((3,)), dma((2,)), dma((2,)), dma((n // 2,)), dma((n // 2,)), dma((m,)), dma((m,)), dma((2, m)), dma((2, m)),
        ],
        compiler_params=pltpu.CompilerParams(
            collective_id=0, has_side_effects=True, vmem_limit_bytes=54400 * 1024
        ),
    )(fractions, ext_table.T, side_table.T, depth_scale.reshape(1, w))
    return jnp.transpose(image, (0, 2, 1))


def solution(mesh):
    return jax.shard_map(
        functools.partial(on_device, mesh.shape["bx"], mesh.shape["cy"]),
        mesh=mesh,
        in_specs=(P(None, "bx", None, "cy"), P(), P(), P()),
        out_specs=P("cy", "bx", None),
        check_vma=False,
    )
```

time: 22.7 us -> 16.3 us (0.72)
  the two profiles are of different devices: /device:TPU:0 before, /device:TPU:4 now
where the time goes in v2:
time: 16.3 us; the launch traced here: 16.2 us
  Pallas kernels  14.8 us (91%)
  local copies, waits for them, and re-layouts  1.33 us (8%)
    pallas_call x1, Pallas kernels, on_device(): pl.pallas_call(functools.partial(kernel, n, m), out_shape=jax.ShapeDtypeS...  14.8 us
    unnamed x7, local copies, waits for them, and re-layouts  1.33 us

profile of v2, /device:TPU:4, one launch (start us, length us, event | category | flops | bytes accessed | tf_op | source)
XLA Modules:
  0.0 16.2 jit_solution(11453757505532886724)
XLA Ops:
  0.0 0.0 copy-start.1
  0.0 0.0 copy-start
  0.0 0.0 copy-start.2
  0.0 0.7 %copy-done.1 = bf16[32,8]{0,1:T(8,128)(2,1)S(1)} copy-done((bf16[32,8]{0,1:T(8,128)(2,1)S(1)}, bf16[32,8]{0,1:T(8,128)(2,1)}, u32[]{:S(2)}) %copy-start.1) | copy-done | bytes 536
  0.7 0.0 copy-done
  0.7 0.0 copy-done.2
  0.7 14.8 %shard_map.46 = f32[8,16,32]{2,1,0:T(8,128)S(1)} custom-call(bf16[8,32,16,128]{3,2,1,0:T(8,128)(2,1)} %f_hbm.1, bf16[8,32]{1,0:T(8,128)(2,1)S(1)} %bitcast.5, bf16[8,32]{1,0:T(8,128)(2,1)S(1)} %bitcast.6, f32[1,32]{1,0:T(1,128)S(1)} %bitcast.7), custom_call_target="tpu_custom_call" | custom-call | tf_op jit(solution)/shard_map/pallas_call | solution.py:309
  15.5 0.6 %copy.6 = f32[8,32,16]{1,2,0:T(8,128)} copy(f32[8,32,16]{1,2,0:T(8,128)S(1)} %bitcast.4) | data formatting | bytes 32768
Async XLA Ops:
  0.0 0.7 %copy-start.1 = (bf16[32,8]{0,1:T(8,128)(2,1)S(1)}, bf16[32,8]{0,1:T(8,128)(2,1)}, u32[]{:S(2)}) copy-start(bf16[32,8]{0,1:T(8,128)(2,1)} %param.6) | copy-start | bytes 1540
  0.0 0.7 %copy-start = (bf16[32,8]{0,1:T(8,128)(2,1)S(1)}, bf16[32,8]{0,1:T(8,128)(2,1)}, u32[]{:S(2)}) copy-start(bf16[32,8]{0,1:T(8,128)(2,1)} %param.5) | copy-start | bytes 1540
  0.0 0.7 %copy-start.2 = (f32[32]{0:T(128)S(1)}, f32[32]{0:T(128)}, u32[]{:S(2)}) copy-start(f32[32]{0:T(128)} %param.7) | copy-start | bytes 388

commit v3 on v2

--- a/solution.py
+++ b/solution.py
@@ -12,8 +12,9 @@
 GROUP = 8
 EARLY = 0
 FIRST = 1
-SECOND = 2
-THIRD = 3
+SECOND = 3
+THIRD = 4
+PARTS = 4
 
 
 def split_halves(value):
@@ -181,7 +182,7 @@
     pair_ref[...] = beam_ref[half] + mate_in[...]
 
     def pair_start(t, c):
-        pair_copy(pair, t).start()
+        pair_copy(pair, pairs + pair - t).start()
         return c
 
     lax.fori_loop(pair + 1, pairs, pair_start, 0)
@@ -211,7 +212,7 @@
     cam_depth = matmul(split_halves(cam), ext_w[...])
     cam_factor = jnp.exp2(cam_depth * factor_ref[:1]) * (1.0 / (cy * m))
     width = wz // m
-    edge = cx // 2
+    edge = cx // PARTS
 
     def img_copy(part, block, slot, t):
         return pltpu.make_async_remote_copy(
@@ -255,19 +256,17 @@
                 img_ref[pl.ds(first, 8), lanes] = jnp.concatenate(rows8, axis=0)
                 return c
 
-            lax.fori_loop(start // 8, stop // 8, eight_x, 0)
-
-    if THIRD * GROUP > edge:
-        finish(edge, THIRD * GROUP)
-    img_start(1)
-    finish(0, min(edge, THIRD * GROUP))
-    img_start(0)
+            lax.fori_loop(start // 8, max(start, stop) // 8, eight_x, 0)
+
+    for part in reversed(range(PARTS)):
+        finish(part * edge, min((part + 1) * edge, THIRD * GROUP))
+        img_start(part)
     total_ref = img_out.at[:, cy_me]
 
     def img_add(j, c):
         @pl.when(j != cy_me)
         def _():
-            for part in (1, 0):
+            for part in reversed(range(PARTS)):
                 img_copy(part, j, j, j).wait_recv()
             total_ref[...] += img_in[:, j]
         return c
@@ -289,7 +288,7 @@
     def img_sent(t, c):
         @pl.when(t != cy_me)
         def _():
-            for part in range(2):
+            for part in range(PARTS):
                 img_copy(part, t, cy_me, t).wait_send()
         return c
 
@@ -326,12 +325,12 @@
             pltpu.VMEM((cx, bz), f32),
             pltpu.VMEM((m, cx, bz), f32),
             pltpu.VMEM((cx, wz), f32),
-            pltpu.VMEM((2, m, cx // 2, width), f32),
-            pltpu.VMEM((2, m, cx // 2, width), f32),
+            pltpu.VMEM((PARTS, m, cx // PARTS, width), f32),
+            pltpu.VMEM((PARTS, m, cx // PARTS, width), f32),
             pltpu.VMEM((2 * bz, wz), bf16),
             pltpu.VMEM((bz, wz), bf16),
             pltpu.VMEM((8, wz), f32),
-            dma, dma((3,)), dma((2,)), dma((2,)), dma((n // 2,)), dma((n // 2,)), dma((m,)), dma((m,)), dma((2, m)), dma((2, m)),
+            dma, dma((3,)), dma((2,)), dma((2,)), dma((n // 2,)), dma((n // 2,)), dma((m,)), dma((m,)), dma((PARTS, m)), dma((PARTS, m)),
         ],
         compiler_params=pltpu.CompilerParams(
             collective_id=0, has_side_effects=True, vmem_limit_bytes=54400 * 1024

time: 16.3 us -> 16.2 us (level)
  the two profiles are of different devices: /device:TPU:4 before, /device:TPU:0 now
where the time goes in v3:
time: 16.2 us; the launch traced here: 16 us
  Pallas kernels  14.7 us (91%)
  local copies, waits for them, and re-layouts  1.33 us (8%)
    pallas_call x1, Pallas kernels, on_device(): pl.pallas_call(functools.partial(kernel, n, m), out_shape=jax.ShapeDtypeS...  14.7 us
    unnamed x7, local copies, waits for them, and re-layouts  1.33 us

profile of v3, /device:TPU:0, one launch (start us, length us, event | category | flops | bytes accessed | tf_op | source)
XLA Modules:
  0.0 16.0 jit_solution(16852410159527392040)
XLA Ops:
  0.0 0.0 copy-start.1
  0.0 0.0 copy-start
  0.0 0.0 copy-start.2
  0.0 0.7 %copy-done.1 = bf16[32,8]{0,1:T(8,128)(2,1)S(1)} copy-done((bf16[32,8]{0,1:T(8,128)(2,1)S(1)}, bf16[32,8]{0,1:T(8,128)(2,1)}, u32[]{:S(2)}) %copy-start.1) | copy-done | bytes 536
  0.7 0.0 copy-done
  0.7 0.0 copy-done.2
  0.7 14.7 %shard_map.46 = f32[8,16,32]{2,1,0:T(8,128)S(1)} custom-call(bf16[8,32,16,128]{3,2,1,0:T(8,128)(2,1)} %f_hbm.1, bf16[8,32]{1,0:T(8,128)(2,1)S(1)} %bitcast.5, bf16[8,32]{1,0:T(8,128)(2,1)S(1)} %bitcast.6, f32[1,32]{1,0:T(1,128)S(1)} %bitcast.7), custom_call_target="tpu_custom_call" | custom-call | tf_op jit(solution)/shard_map/pallas_call | solution.py:308
  15.4 0.6 %copy.6 = f32[8,32,16]{1,2,0:T(8,128)} copy(f32[8,32,16]{1,2,0:T(8,128)S(1)} %bitcast.4) | data formatting | bytes 32768
Async XLA Ops:
  0.0 0.7 %copy-start.1 = (bf16[32,8]{0,1:T(8,128)(2,1)S(1)}, bf16[32,8]{0,1:T(8,128)(2,1)}, u32[]{:S(2)}) copy-start(bf16[32,8]{0,1:T(8,128)(2,1)} %param.6) | copy-start | bytes 1540
  0.0 0.7 %copy-start = (bf16[32,8]{0,1:T(8,128)(2,1)S(1)}, bf16[32,8]{0,1:T(8,128)(2,1)}, u32[]{:S(2)}) copy-start(bf16[32,8]{0,1:T(8,128)(2,1)} %param.5) | copy-start | bytes 1540
  0.0 0.7 %copy-start.2 = (f32[32]{0:T(128)S(1)}, f32[32]{0:T(128)}, u32[]{:S(2)}) copy-start(f32[32]{0:T(128)} %param.7) | copy-start | bytes 388
